TPU v7x, 512 devices: a whole 4x4x16 slice. The times are simulated.
512 devices in a mesh: row: 16 (over z_lo, x), col: 32 (over y, z_hi, core).
Axes of the slice: x: 4, y: 4, z: 16 (z_hi: 4, z_lo: 4; z = z_hi * 4 + z_lo), core: 2. Of those that a mesh axis runs over, the one named last changes fastest.
Arguments:
- x_cols: bfloat16 [8, 262144], P(None, ('col', 'row')), may hold values from -6 to 6
- diag_rows: float32 [262144], P(('row', 'col')), may hold values from 0.5 to 2
- theta: float32 [8], replicated, may hold values from -1 to 1
- tiles: bfloat16 [16, 32, 96, 128, 128], P('row', 'col'), may hold values from -0.109375 to 0.109375
- tile_rows: int32 [16, 32, 96], P('row', 'col'), may hold values from 0 to 127, as said below
- tile_cols: int32 [16, 32, 96], P('row', 'col'), may hold values from 0 to 63, as said below
- counts: int32 [16, 32], P('row', 'col'), may hold values from 48 to 96, as said below
Outputs:
- resid: float32 [8, 262144], P(None, ('row', 'col'))
- image: float32 [8, 262144], P(None, ('col', 'row'))
Inputs may be any that keep to these rules, and one draw needn't show every extreme that they name: Within one device block, the pairs (tile_rows, tile_cols) of its 96 slots are all different. `tile_cols`: paired with tile_rows slot by slot. `counts`: slots at or past a block's count are unused and their tiles hold arbitrary values. Some block has all 96 slots in use.
All inputs are finite; a program needn't handle non-finite values.
Results may differ from a plain program's by a relative error of at most 0.0023.
Values may be sent and summed in bfloat16 or wider, within the bound.
No kernel may reach another device: no remote copies, remote signals or barrier semaphores. Data moves between devices by JAX's collectives and lax.ppermute only.
A program may use at most 64 MiB of HBM per device.

v0:
```python
import jax
import jax.numpy as jnp
from jax import lax
from jax.sharding import PartitionSpec as P


def flatten_blocks(blocks):
    return blocks.transpose(1, 0, 2).reshape(blocks.shape[1], -1)


def body(x_cols, diag_rows, theta, tiles, tile_rows, tile_cols, counts):
    row_devices = lax.axis_size("row")
    column_devices = lax.axis_size("col")
    fold_ratio = column_devices // row_devices
    vectors = x_cols.shape[0]
    own_states = x_cols.shape[1]
    blocks_here = tiles[0, 0]
    rows_here = tile_rows[0, 0]
    cols_here = tile_cols[0, 0]
    slot_count = blocks_here.shape[0]
    tile_width = blocks_here.shape[1]
    in_use = jnp.arange(slot_count, dtype=jnp.int32) < counts[0, 0]
    block_rows = own_states * column_devices // tile_width
    block_cols = own_states * row_devices // tile_width
    share_rows = own_states // tile_width
    column_vectors = lax.all_gather(x_cols, "row", axis=1, tiled=True)
    column_tiles = column_vectors.reshape(vectors, block_cols, tile_width).transpose(1, 0, 2)
    picked = jnp.take(column_tiles, cols_here, axis=0)
    products = jnp.einsum("kab,knb->kna", blocks_here, picked, preferred_element_type=jnp.float32)
    products = jnp.where(in_use[:, None, None], products, 0.0)
    partial_value = jax.ops.segment_sum(products, rows_here, num_segments=block_rows)
    on_diag = (lax.axis_index("row") == lax.axis_index("col") // fold_ratio).astype(jnp.float32)
    offset = lax.axis_index("col") % fold_ratio * block_cols
    shift_term = -theta[None, :, None] * column_tiles.astype(jnp.float32) * on_diag
    current = lax.dynamic_slice_in_dim(partial_value, offset, block_cols, 0)
    partial_value = lax.dynamic_update_slice_in_dim(partial_value, current + shift_term, offset, 0)
    scales = lax.all_gather(diag_rows, "col", axis=0, tiled=True)
    summed = lax.psum(partial_value, "col")
    scaled = (summed / scales.reshape(-1, 1, tile_width)).astype(jnp.bfloat16)
    resid_part = lax.dynamic_slice_in_dim(summed, lax.axis_index("col") * share_rows, share_rows, 0)
    picked_rows = jnp.take(scaled, rows_here, axis=0)
    transposed = jnp.einsum(
        "kab,kna->knb", blocks_here, picked_rows, preferred_element_type=jnp.float32
    )
    transposed = jnp.where(in_use[:, None, None], transposed, 0.0)
    partial_back = jax.ops.segment_sum(transposed, cols_here, num_segments=block_cols)
    image_part = lax.psum_scatter(partial_back, "row", scatter_dimension=0, tiled=True)
    return (flatten_blocks(resid_part), flatten_blocks(image_part))


def solution(mesh):
    return jax.shard_map(
        body,
        mesh=mesh,
        in_specs=(
            P(None, ("col", "row")),
            P(("row", "col")),
            P(),
            P("row", "col", None, None, None),
            P("row", "col", None),
            P("row", "col", None),
            P("row", "col"),
        ),
        out_specs=(P(None, ("row", "col")), P(None, ("col", "row"))),
        check_vma=False,
    )
```

profile of v0, /device:TPU:8, one launch (start us, length us, event | category | flops | bytes accessed | tf_op | source)
XLA Modules:
  0.0 519.1 jit_solution(790691710098318919)
XLA Ops:
  7.2 0.0 copy-start
  7.2 0.0 copy-start.4
  7.2 0.0 all-reduce.2.cloned.1.call-start
  7.2 44.6 %all_gather.6 = bf16[8,8192]{1,0:T(8,128)(2,1)S(1)} all-gather(bf16[8,512]{1,0:T(8,128)(2,1)} %param.7), channel_id=1, replica_groups=mesh['row'=16,'col'=32] {'row'}, dimensions={1}, use_global_device_ids=true | all-gather | bytes 139264 | tf_op jit(solution)/shard_map/all_gather | solution.py:26
  51.8 0.7 fusion.16
  53.1 0.7 compare_and_fusion.1
  53.8 0.7 neg.4
  54.5 0.7 gather_fusion
  55.1 0.0 copy-done
  55.1 0.0 copy-start.3
  55.2 2.5 fusion.4
  57.7 0.8 broadcast_in_dim.43
  58.5 0.0 copy-done.4
  58.5 10.8 %scatter_fusion = f32[128,8,128]{2,1,0:T(8,128)} fusion(f32[128,8,128]{2,1,0:T(8,128)} %broadcast_in_dim.43, s32[96]{0:T(128)S(1)} %bitcast.40, f32[96,8,128]{2,1,0:T(8,128)} %fusion.4), kind=kCustom, calls=%fused_computation.2 | custom fusion | flops 98304 | bytes 1180032 | tf_op jit(solution)/shard_map/scatter-add | solution.py:31
  69.3 0.0 copy-start.2
  69.3 1.8 add_dynamic-update-slice_fusion
  71.1 0.0 all-reduce.2.cloned.1.call-update
  71.1 0.0 reduce-scatter.2.cloned.1.call-start
  71.2 0.0 copy-done.3
  71.2 52.4 %all-gather = f32[32,1,512]{2,1,0:T(1,128)S(1)} all-gather(f32[1,1,512]{2,1,0:T(1,128)S(1)} %bitcast.39), channel_id=1, replica_groups=mesh['row'=16,'col'=32] {'col'}, dimensions={0}, use_global_device_ids=true | all-gather | bytes 67584 | tf_op jit(solution)/shard_map/all_gather | solution.py:37
  123.6 278.2 %all-reduce.2.cloned.1.call-done = f32[128,8,128]{2,1,0:T(8,128)} async-done(((f32[128,8,128]{2,1,0:T(8,128)}), f32[128,8,128]{2,1,0:T(8,128)}) %all-reduce.2.cloned.1.call-update) | async-done | bytes 524304 | tf_op jit(solution)/shard_map/psum | solution.py:38
  401.8 1.1 divide_convert_fusion
  402.9 1.3 gather_fusion.1
  404.3 2.7 fusion.7
  407.0 0.0 copy-done.2
  407.0 7.3 %scatter_fusion.1 = f32[64,8,128]{2,1,0:T(8,128)S(1)} fusion(f32[64,8,128]{2,1,0:T(8,128)S(1)} %broadcast_in_dim.48, s32[96]{0:T(128)S(1)} %bitcast.38, f32[96,8,128]{2,1,0:T(8,128)} %fusion.7), kind=kCustom, calls=%fused_computation.3 | custom fusion | flops 98304 | bytes 1180032 | tf_op jit(solution)/shard_map/scatter-add | solution.py:46
  414.2 0.0 copy-start.1
  414.3 0.7 copy-done.1
  414.9 0.0 reduce-scatter.2.cloned.1.call-update
  415.0 1.3 dynamic-slice_bitcast_fusion
  416.3 96.0 %reduce-scatter.2.cloned.1.call-done = f32[4,8,128]{2,1,0:T(8,128)} async-done(((f32[64,8,128]{2,1,0:T(8,128)}), f32[4,8,128]{2,1,0:T(8,128)}) %reduce-scatter.2.cloned.1.call-update) | async-done | bytes 16400 | tf_op jit(solution)/shard_map/reduce_scatter | solution.py:47
  (5 shorter events, 0.0 us)
Async XLA Ops:
  7.2 48.0 %copy-start = (bf16[1,1,96,128,128]{4,3,2,1,0:T(8,128)(2,1)S(1)}, bf16[1,1,96,128,128]{4,3,2,1,0:T(8,128)(2,1)}, u32[]{:S(2)}) copy-start(bf16[1,1,96,128,128]{4,3,2,1,0:T(8,128)(2,1)} %param.10) | copy-start | bytes 9437188
  7.2 51.3 %copy-start.4 = (s32[1,1,96]{2,1,0:T(1,128)S(1)}, s32[1,1,96]{2,1,0:T(1,128)}, u32[]{:S(2)}) copy-start(s32[1,1,96]{2,1,0:T(1,128)} %param.11) | copy-start | bytes 1156
  7.2 394.6 %all-reduce.2.cloned.1.call-start = ((), (), s32[]{:S(2)}) async-start(), calls=%async_computation.1 | async-start | bytes 1048576 | tf_op jit(solution)/shard_map/psum | solution.py:38
  55.1 16.0 %copy-start.3 = (f32[512]{0:T(512)S(1)}, f32[512]{0:T(512)}, u32[]{:S(2)}) copy-start(f32[512]{0:T(512)} %param.8) | copy-start | bytes 6148
  69.3 337.6 %copy-start.2 = (s32[1,1,96]{2,1,0:T(1,128)S(1)}, s32[1,1,96]{2,1,0:T(1,128)}, u32[]{:S(2)}) copy-start(s32[1,1,96]{2,1,0:T(1,128)} %param.12) | copy-start | bytes 1156
  71.1 441.2 %reduce-scatter.2.cloned.1.call-start = ((), (), s32[]{:S(2)}) async-start(), calls=%async_computation.2 | async-start | bytes 278528 | tf_op jit(solution)/shard_map/reduce_scatter | solution.py:47
  414.2 0.7 copy-start.1
Sparse Core Ops, SparseCore 0:
  71.2 330.5 all-reduce.1
  415.1 97.1 reduce-scatter.1
where the time goes:
time: 520 us; the launch traced here: 519 us
  waiting for transfers between devices  374 us (72%)
  blocking collectives  97 us (19%)
  other arithmetic  23 us (4%)
  between operations  14.8 us (3%)
    psum x1, waiting for transfers between devices, body(): summed = lax.psum(partial_value, 'col')  278 us
    reduce_scatter x1, waiting for transfers between devices, body(): lax.psum_scatter(partial_back, 'row', scatter_dimension=0, tiled=True)  96 us
    all_gather x1, blocking collectives, body(): scales = lax.all_gather(diag_rows, 'col', axis=0, tiled=True)  52.4 us
    all_gather x1, blocking collectives, body(): column_vectors = lax.all_gather(x_cols, 'row', axis=1, tiled=True)  44.6 us
    scatter-add x1, other arithmetic, body(): jax.ops.segment_sum(products, rows_here, num_segments=block_rows)  10.8 us
  transfers between devices with their start and end apart: 2, of which 2 were waited for; matrix products, arithmetic and copies ran while one was open for 0% of the time, Pallas kernels for 0%

commit v1 on v0

--- a/solution.py
+++ b/solution.py
@@ -34,7 +34,9 @@
     shift_term = -theta[None, :, None] * column_tiles.astype(jnp.float32) * on_diag
     current = lax.dynamic_slice_in_dim(partial_value, offset, block_cols, 0)
     partial_value = lax.dynamic_update_slice_in_dim(partial_value, current + shift_term, offset, 0)
-    scales = lax.all_gather(diag_rows, "col", axis=0, tiled=True)
+    scales = jnp.concatenate(
+        lax.all_to_all(jnp.stack([diag_rows] * lax.axis_size("col")), "col", 0, 0), axis=0
+    )
     summed = lax.psum(partial_value, "col")
     scaled = (summed / scales.reshape(-1, 1, tile_width)).astype(jnp.bfloat16)
     resid_part = lax.dynamic_slice_in_dim(summed, lax.axis_index("col") * share_rows, share_rows, 0)

time: 520 us -> 520 us (level)
  blocking collectives: 97 us -> 44.6 us
  waiting for transfers between devices: 374 us -> 410 us
  starting transfers between devices: 0.08 us -> 15.7 us
    all_gather x1 -> x0, blocking collectives: 52.4 us -> none  [body(): scales = lax.all_gather(diag_rows, 'col', axis=0, tiled=True)]
    psum x1, waiting for transfers between devices: 278 us -> 301 us  [body(): summed = lax.psum(partial_value, 'col')]
    all_to_all x0 -> x1, starting transfers between devices: none -> 15.6 us  [body(): lax.all_to_all(jnp.stack([diag_rows] * lax.axis_size('col')), 'col', 0, 0)]
    all_to_all x0 -> x1, waiting for transfers between devices: none -> 13.5 us  [body(): lax.all_to_all(jnp.stack([diag_rows] * lax.axis_size('col')), 'col', 0, 0)]
  transfers between devices with their start and end apart: 2 -> 3, of which waited for: 2 -> 3; matrix products, arithmetic and copies ran while one was open for 0% -> 0% of each run, Pallas kernels for 0% -> 0%
where the time goes in v1:
time: 520 us; the launch traced here: 519 us
  waiting for transfers between devices  410 us (79%)
  blocking collectives  44.6 us (9%)
  other arithmetic  22.9 us (4%)
  starting transfers between devices  15.7 us (3%)
  between operations  14.8 us (3%)
  local copies, waits for them, and re-layouts  5.54 us (1%)
    psum x1, waiting for transfers between devices, body(): summed = lax.psum(partial_value, 'col')  301 us
    reduce_scatter x1, waiting for transfers between devices, body(): lax.psum_scatter(partial_back, 'row', scatter_dimension=0, tiled=True)  95.9 us
    all_gather x1, blocking collectives, body(): column_vectors = lax.all_gather(x_cols, 'row', axis=1, tiled=True)  44.6 us
    all_to_all x1, starting transfers between devices, body(): lax.all_to_all(jnp.stack([diag_rows] * lax.axis_size('col')), 'col', 0, 0)  15.6 us
    all_to_all x1, waiting for transfers between devices, body(): lax.all_to_all(jnp.stack([diag_rows] * lax.axis_size('col')), 'col', 0, 0)  13.5 us
    scatter-add x1, other arithmetic, body(): jax.ops.segment_sum(products, rows_here, num_segments=block_rows)  10.8 us
  transfers between devices with their start and end apart: 3, of which 3 were waited for; matrix products, arithmetic and copies ran while one was open for 0% of the time, Pallas kernels for 0%

profile of v1, /device:TPU:8, one launch (start us, length us, event | category | flops | bytes accessed | tf_op | source)
XLA Modules:
  0.0 519.1 jit_solution(16784262700681945723)
XLA Ops:
  7.2 0.0 copy-start
  7.2 0.0 copy-start.4
  7.2 0.0 all-reduce.2.cloned.1.call-start
  7.2 44.6 %all_gather.3 = bf16[8,8192]{1,0:T(8,128)(2,1)S(1)} all-gather(bf16[8,512]{1,0:T(8,128)(2,1)} %param.7), channel_id=1, replica_groups=mesh['row'=16,'col'=32] {'row'}, dimensions={1}, use_global_device_ids=true | all-gather | bytes 139264 | tf_op jit(solution)/shard_map/all_gather | solution.py:26
  51.8 0.7 fusion.16
  53.1 0.7 compare_and_fusion.1
  53.8 0.7 neg.4
  54.5 0.7 gather_fusion
  55.1 0.0 copy-done
  55.1 0.0 copy-start.3
  55.2 2.5 fusion.4
  57.7 0.8 broadcast_in_dim.43
  58.5 0.0 copy-done.4
  58.5 10.8 %scatter_fusion = f32[128,8,128]{2,1,0:T(8,128)} fusion(f32[128,8,128]{2,1,0:T(8,128)} %broadcast_in_dim.43, s32[96]{0:T(128)S(1)} %bitcast.38, f32[96,8,128]{2,1,0:T(8,128)} %fusion.4), kind=kCustom, calls=%fused_computation.2 | custom fusion | flops 98304 | bytes 1180032 | tf_op jit(solution)/shard_map/scatter-add | solution.py:31
  69.3 1.7 add_dynamic-update-slice_fusion
  71.1 0.0 copy-start.2
  71.1 0.0 all-reduce.2.cloned.1.call-update
  71.1 0.0 copy-done.3
  71.1 0.7 stack.2
  71.8 15.6 %all-to-all-start = ((f32[32,1,512]{2,1,0:T(1,128)}), f32[32,1,512]{2,1,0:T(1,128)S(1)}, u32[]{:S(2)}, u32[]{:S(2)}) async-start(f32[32,1,512]{2,1,0:T(1,128)} %stack.2), calls=%async_computation | async-start | bytes 131072 | tf_op jit(solution)/shard_map/all_to_all | solution.py:38
  87.4 0.0 reduce-scatter.2.cloned.1.call-start
  87.5 13.5 %all-to-all-done = f32[32,1,512]{2,1,0:T(1,128)S(1)} async-done(((f32[32,1,512]{2,1,0:T(1,128)}), f32[32,1,512]{2,1,0:T(1,128)S(1)}, u32[]{:S(2)}, u32[]{:S(2)}) %all-to-all-start) | async-done | bytes 65568 | tf_op jit(solution)/shard_map/all_to_all | solution.py:38
  101.0 300.9 %all-reduce.2.cloned.1.call-done = f32[128,8,128]{2,1,0:T(8,128)} async-done(((f32[128,8,128]{2,1,0:T(8,128)}), f32[128,8,128]{2,1,0:T(8,128)}) %all-reduce.2.cloned.1.call-update) | async-done | bytes 524304 | tf_op jit(solution)/shard_map/psum | solution.py:40
  401.9 1.1 divide_convert_fusion
  403.0 1.3 gather_fusion.1
  404.4 2.6 fusion.7
  407.0 0.0 copy-done.2
  407.0 7.3 %scatter_fusion.1 = f32[64,8,128]{2,1,0:T(8,128)S(1)} fusion(f32[64,8,128]{2,1,0:T(8,128)S(1)} %broadcast_in_dim.48, s32[96]{0:T(128)S(1)} %bitcast.37, f32[96,8,128]{2,1,0:T(8,128)} %fusion.7), kind=kCustom, calls=%fused_computation.3 | custom fusion | flops 98304 | bytes 1180032 | tf_op jit(solution)/shard_map/scatter-add | solution.py:48
  414.3 0.0 copy-start.1
  414.3 0.7 copy-done.1
  415.0 0.0 reduce-scatter.2.cloned.1.call-update
  415.0 1.3 dynamic-slice_bitcast_fusion
  416.4 95.9 %reduce-scatter.2.cloned.1.call-done = f32[4,8,128]{2,1,0:T(8,128)} async-done(((f32[64,8,128]{2,1,0:T(8,128)}), f32[4,8,128]{2,1,0:T(8,128)}) %reduce-scatter.2.cloned.1.call-update) | async-done | bytes 16400 | tf_op jit(solution)/shard_map/reduce_scatter | solution.py:49
  (5 shorter events, 0.0 us)
Async XLA Ops:
  7.2 48.0 %copy-start = (bf16[1,1,96,128,128]{4,3,2,1,0:T(8,128)(2,1)S(1)}, bf16[1,1,96,128,128]{4,3,2,1,0:T(8,128)(2,1)}, u32[]{:S(2)}) copy-start(bf16[1,1,96,128,128]{4,3,2,1,0:T(8,128)(2,1)} %param.10) | copy-start | bytes 9437188
  7.2 51.3 %copy-start.4 = (s32[1,1,96]{2,1,0:T(1,128)S(1)}, s32[1,1,96]{2,1,0:T(1,128)}, u32[]{:S(2)}) copy-start(s32[1,1,96]{2,1,0:T(1,128)} %param.11) | copy-start | bytes 1156
  7.2 394.7 %all-reduce.2.cloned.1.call-start = ((), (), s32[]{:S(2)}) async-start(), calls=%async_computation.2 | async-start | bytes 1048576 | tf_op jit(solution)/shard_map/psum | solution.py:40
  55.1 16.0 %copy-start.3 = (f32[512]{0:T(512)S(1)}, f32[512]{0:T(512)}, u32[]{:S(2)}) copy-start(f32[512]{0:T(512)} %param.8) | copy-start | bytes 6148
  71.1 335.9 %copy-start.2 = (s32[1,1,96]{2,1,0:T(1,128)S(1)}, s32[1,1,96]{2,1,0:T(1,128)}, u32[]{:S(2)}) copy-start(s32[1,1,96]{2,1,0:T(1,128)} %param.12) | copy-start | bytes 1156
  71.8 29.2 %all-to-all-start = ((f32[32,1,512]{2,1,0:T(1,128)}), f32[32,1,512]{2,1,0:T(1,128)S(1)}, u32[]{:S(2)}, u32[]{:S(2)}) async-start(f32[32,1,512]{2,1,0:T(1,128)} %stack.2), calls=%async_computation | async-start | bytes 131072 | tf_op jit(solution)/shard_map/all_to_all | solution.py:38
  87.4 424.9 %reduce-scatter.2.cloned.1.call-start = ((), (), s32[]{:S(2)}) async-start(), calls=%async_computation.3 | async-start | bytes 278528 | tf_op jit(solution)/shard_map/reduce_scatter | solution.py:49
  414.3 0.7 copy-start.1
Sparse Core Ops, SparseCore 0:
  71.2 330.6 all-reduce.1
  415.1 97.1 reduce-scatter.1

commit v2 on v0

--- a/solution.py
+++ b/solution.py
@@ -35,7 +35,7 @@
     current = lax.dynamic_slice_in_dim(partial_value, offset, block_cols, 0)
     partial_value = lax.dynamic_update_slice_in_dim(partial_value, current + shift_term, offset, 0)
     scales = lax.all_gather(diag_rows, "col", axis=0, tiled=True)
-    summed = lax.psum(partial_value, "col")
+    summed = jnp.sum(lax.all_gather(partial_value, "col"), axis=0)
     scaled = (summed / scales.reshape(-1, 1, tile_width)).astype(jnp.bfloat16)
     resid_part = lax.dynamic_slice_in_dim(summed, lax.axis_index("col") * share_rows, share_rows, 0)
     picked_rows = jnp.take(scaled, rows_here, axis=0)

time: 520 us -> 404 us (0.78)
  waiting for transfers between devices: 374 us -> 243 us
  other arithmetic: 23 us -> 29.7 us
  blocking collectives: 97 us -> 103 us
    psum x1 -> x0, waiting for transfers between devices: 278 us -> none  [body(): summed = lax.psum(partial_value, 'col')]
    all_gather x0 -> x1, waiting for transfers between devices: none -> 160 us  [body(): summed = jnp.sum(lax.all_gather(partial_value, 'col'), axis=0)]
    reduce_scatter x1, waiting for transfers between devices: 96 us -> 82.9 us  [body(): lax.psum_scatter(partial_back, 'row', scatter_dimension=0, tiled=True)]
    reduce_sum x0 -> x1, other arithmetic: none -> 7.35 us  [body(): summed = jnp.sum(lax.all_gather(partial_value, 'col'), axis=0)]
    all_gather x1, blocking collectives: 52.4 us -> 58.7 us  [body(): scales = lax.all_gather(diag_rows, 'col', axis=0, tiled=True)]
where the time goes in v2:
time: 404 us; the launch traced here: 403 us
  waiting for transfers between devices  243 us (60%)
  blocking collectives  103 us (25%)
  other arithmetic  29.7 us (7%)
  between operations  15 us (4%)
  local copies, waits for them, and re-layouts  6.72 us (2%)
  matrix products  5.17 us (1%)
    all_gather x1, waiting for transfers between devices, body(): summed = jnp.sum(lax.all_gather(partial_value, 'col'), axis=0)  160 us
    reduce_scatter x1, waiting for transfers between devices, body(): lax.psum_scatter(partial_back, 'row', scatter_dimension=0, tiled=True)  82.9 us
    all_gather x1, blocking collectives, body(): scales = lax.all_gather(diag_rows, 'col', axis=0, tiled=True)  58.7 us
    all_gather x1, blocking collectives, body(): column_vectors = lax.all_gather(x_cols, 'row', axis=1, tiled=True)  44.4 us
    scatter-add x1, other arithmetic, body(): jax.ops.segment_sum(products, rows_here, num_segments=block_rows)  10.8 us
  transfers between devices with their start and end apart: 2, of which 2 were waited for; matrix products, arithmetic and copies ran while one was open for 0% of the time, Pallas kernels for 0%

profile of v2, /device:TPU:8, one launch (start us, length us, event | category | flops | bytes accessed | tf_op | source)
XLA Modules:
  0.0 402.7 jit_solution(8119994197836884782)
XLA Ops:
  7.2 0.0 copy-start
  7.2 0.0 copy-start.4
  7.2 0.0 all-gather.3.cloned.1.call-start
  8.1 0.7 fusion.16
  8.8 0.7 compare_and_fusion.1
  9.5 44.4 %all_gather.14 = bf16[8,8192]{1,0:T(8,128)(2,1)S(1)} all-gather(bf16[8,512]{1,0:T(8,128)(2,1)} %param.7), channel_id=1, replica_groups=mesh['row'=16,'col'=32] {'row'}, dimensions={1}, use_global_device_ids=true | all-gather | bytes 139264 | tf_op jit(solution)/shard_map/all_gather | solution.py:26
  53.9 0.7 gather_fusion
  54.6 0.0 copy-done
  54.6 0.0 copy-start.5
  54.6 0.0 copy-start.3
  54.6 2.5 fusion.4
  57.1 0.8 broadcast_in_dim.43
  57.9 0.0 copy-done.4
  57.9 10.8 %scatter_fusion = f32[128,8,128]{2,1,0:T(8,128)} fusion(f32[128,8,128]{2,1,0:T(8,128)} %broadcast_in_dim.43, s32[96]{0:T(128)S(1)} %bitcast.44, f32[96,8,128]{2,1,0:T(8,128)} %fusion.4), kind=kCustom, calls=%fused_computation.2 | custom fusion | flops 98304 | bytes 1180032 | tf_op jit(solution)/shard_map/scatter-add | solution.py:31
  68.7 1.9 copy.10
  70.6 0.0 copy-done.5
  70.6 1.8 bitcast_dynamic-update-slice_fusion
  72.4 0.0 all-gather.3.cloned.1.call-update
  72.4 0.0 reduce-scatter.2.cloned.1.call-start
  72.4 0.0 copy-done.3
  72.4 58.7 %all-gather = f32[32,1,512]{2,1,0:T(1,128)S(1)} all-gather(f32[1,1,512]{2,1,0:T(1,128)S(1)} %bitcast.43), channel_id=1, replica_groups=mesh['row'=16,'col'=32] {'col'}, dimensions={0}, use_global_device_ids=true | all-gather | bytes 67584 | tf_op jit(solution)/shard_map/all_gather | solution.py:37
  131.1 160.0 %all-gather.3.cloned.1.call-done = f32[32,128,8,128]{3,2,1,0:T(8,128)} async-done(((f32[1,128,8,128]{3,2,1,0:T(8,128)}), f32[32,128,8,128]{3,2,1,0:T(8,128)}) %all-gather.3.cloned.1.call-update) | async-done | bytes 16777232 | tf_op jit(solution)/shard_map/all_gather | solution.py:38
  291.2 7.3 %reduce_sum.9 = f32[128,8,128]{2,1,0:T(8,128)} reduce(f32[32,128,8,128]{3,2,1,0:T(8,128)} %all-gather.3.cloned.1.call-done, f32[]{:T(128)} %constant.58.clone.1), dimensions={0}, to_apply=%region_1.2 | reduce | flops 4063232 | bytes 17301508 | tf_op jit(solution)/shard_map/reduce_sum | solution.py:38
  298.5 0.0 copy-start.2
  298.5 1.1 divide_convert_fusion
  299.7 1.3 gather_fusion.1
  301.0 2.7 fusion.7
  303.7 0.0 copy-done.2
  303.7 7.3 %scatter_fusion.1 = f32[64,8,128]{2,1,0:T(8,128)S(1)} fusion(f32[64,8,128]{2,1,0:T(8,128)S(1)} %broadcast_in_dim.48, s32[96]{0:T(128)S(1)} %bitcast.42, f32[96,8,128]{2,1,0:T(8,128)} %fusion.7), kind=kCustom, calls=%fused_computation.3 | custom fusion | flops 98304 | bytes 1180032 | tf_op jit(solution)/shard_map/scatter-add | solution.py:46
  310.9 0.0 copy-start.1
  310.9 0.7 copy-done.1
  311.6 0.0 reduce-scatter.2.cloned.1.call-update
  311.7 1.3 dynamic-slice_bitcast_fusion
  313.0 82.9 %reduce-scatter.2.cloned.1.call-done = f32[4,8,128]{2,1,0:T(8,128)} async-done(((f32[64,8,128]{2,1,0:T(8,128)}), f32[4,8,128]{2,1,0:T(8,128)}) %reduce-scatter.2.cloned.1.call-update) | async-done | bytes 16400 | tf_op jit(solution)/shard_map/reduce_scatter | solution.py:47
  (6 shorter events, 0.0 us)
Async XLA Ops:
  7.2 47.4 %copy-start = (bf16[1,1,96,128,128]{4,3,2,1,0:T(8,128)(2,1)S(1)}, bf16[1,1,96,128,128]{4,3,2,1,0:T(8,128)(2,1)}, u32[]{:S(2)}) copy-start(bf16[1,1,96,128,128]{4,3,2,1,0:T(8,128)(2,1)} %param.10) | copy-start | bytes 9437188
  7.2 50.8 %copy-start.4 = (s32[1,1,96]{2,1,0:T(1,128)S(1)}, s32[1,1,96]{2,1,0:T(1,128)}, u32[]{:S(2)}) copy-start(s32[1,1,96]{2,1,0:T(1,128)} %param.11) | copy-start | bytes 1156
  7.2 284.0 %all-gather.3.cloned.1.call-start = ((), (), s32[]{:S(2)}) async-start(), calls=%async_computation.1 | async-start | bytes 17301504 | tf_op jit(solution)/shard_map/all_gather | solution.py:38
  54.6 16.0 %copy-start.5 = (f32[8]{0:T(128)S(1)}, f32[8]{0:T(128)}, u32[]{:S(2)}) copy-start(f32[8]{0:T(128)} %param.9) | copy-start | bytes 100
  54.6 17.8 %copy-start.3 = (f32[512]{0:T(512)S(1)}, f32[512]{0:T(512)}, u32[]{:S(2)}) copy-start(f32[512]{0:T(512)} %param.8) | copy-start | bytes 6148
  72.4 323.5 %reduce-scatter.2.cloned.1.call-start = ((), (), s32[]{:S(2)}) async-start(), calls=%async_computation.2 | async-start | bytes 278528 | tf_op jit(solution)/shard_map/reduce_scatter | solution.py:47
  298.5 5.1 %copy-start.2 = (s32[1,1,96]{2,1,0:T(1,128)S(1)}, s32[1,1,96]{2,1,0:T(1,128)}, u32[]{:S(2)}) copy-start(s32[1,1,96]{2,1,0:T(1,128)} %param.12) | copy-start | bytes 1156
  310.9 0.7 copy-start.1
Sparse Core Ops, SparseCore 0:
  72.5 218.6 all-gather.2
  311.8 84.0 reduce-scatter.1
